TPU v7x, 32 devices: a whole 2x2x4 slice. The times are simulated.
32 devices in a mesh: inst: 16 (over z, y, core), tp: 2 (over x).
Axes of the slice: x: 2, y: 2, z: 4, core: 2. Of those that a mesh axis runs over, the one named last changes fastest.
Arguments:
- hidden_state: bfloat16 [2048, 6144], P('inst', 'tp'), may hold values from -3000 to 3000
- norm_gain: bfloat16 [6144], P('tp'), may hold values from 0.099609375 to 1.8984375
- kv_weight: bfloat16 [6144, 8, 256], P('tp'), may hold values from -0.078125 to 0.078125
- queries: bfloat16 [2048, 48, 128], P('inst', 'tp'), may hold values from -120 to 120
- pool_keys: bfloat16 [320, 8, 128, 128], P('inst', 'tp'), may hold values from -6 to 6
- pool_values: bfloat16 [320, 8, 128, 128], P('inst', 'tp'), may hold values from -6 to 6
- page_table: int32 [2048, 12], P('inst'), may hold values from 0 to 19, as said below
- lengths: int32 [2048], P('inst'), may hold values from 2 to 1536
- move_target: int32 [128, 1], P('inst'), may hold values from 0 to 15; in each aligned block of 8 rows (0 to 7, 8 to 15, ...) no two rows name the same one
- move_page: int32 [128], P('inst'), may hold values from 0 to 19
- move_request: int32 [128], P('inst'), may hold values from 0 to 127
Outputs:
- attention_out: bfloat16 [2048, 6144], P('inst', 'tp')
- new_kv: bfloat16 [2048, 8, 256], P('inst', 'tp')
Inputs may be any that keep to these rules, and one draw needn't show every extreme that they name: `page_table`: each row names 12 distinct pages of its instance's pool. `move_target`: the 8 rows of one instance never name the same destination twice.
All inputs are finite; a program needn't handle non-finite values.
Results may differ from a plain program's by a relative error of at most 0.005.
Values may be sent and summed in bfloat16 or wider, within the bound.
A program may use at most 128 MiB of HBM per device.

v0:
```python
import math

import jax
import jax.numpy as jnp
from jax import lax
from jax.sharding import PartitionSpec as P

EPSILON = 1e-05
ROPE_BASE = 1000000.0
FLOOR_SCORE = -1e30


def rotate_keys(key_rows, positions):
    half_width = key_rows.shape[-1] // 2
    freq_steps = jnp.arange(half_width, dtype=jnp.float32)
    frequency = ROPE_BASE ** (-2.0 * freq_steps / key_rows.shape[-1])
    angles = positions.astype(jnp.float32)[:, None, None] * frequency[None, None, :]
    first_half = key_rows[..., :half_width]
    second_half = key_rows[..., half_width:]
    cosine = jnp.cos(angles)
    sine_part = jnp.sin(angles)
    return jnp.concatenate(
        [
            first_half * cosine - second_half * sine_part,
            second_half * cosine + first_half * sine_part,
        ],
        axis=-1,
    )


def page_blocks(query_rows, key_pages, value_pages, scaling):
    scores = (
        jnp.einsum("ngqd,ngtd->ngqt", query_rows, key_pages, preferred_element_type=jnp.float32)
        * scaling
    )
    highest = jnp.max(scores, axis=-1)
    weights = jnp.exp(scores - highest[..., None])
    block_sum = jnp.sum(weights, axis=-1)
    block_out = jnp.einsum(
        "ngqt,ngtd->ngqd",
        weights.astype(jnp.bfloat16),
        value_pages,
        preferred_element_type=jnp.float32,
    )
    return (highest, block_sum, block_out)


def body(
    hidden_state,
    norm_gain,
    kv_weight,
    queries,
    pool_keys,
    pool_values,
    page_table,
    lengths,
    move_target,
    move_page,
    move_request,
):
    widened = hidden_state.astype(jnp.float32)
    squares = lax.psum(jnp.sum(widened * widened, axis=1), "tp")
    features = hidden_state.shape[1] * lax.axis_size("tp")
    inverse = lax.rsqrt(squares / features + EPSILON)
    normed = (widened * inverse[:, None] * norm_gain.astype(jnp.float32)[None, :]).astype(
        jnp.bfloat16
    )
    projected = jnp.transpose(
        lax.psum_scatter(
            jnp.einsum("rf,fgc->grc", normed, kv_weight, preferred_element_type=jnp.float32),
            "tp",
            scatter_dimension=0,
            tiled=True,
        ),
        (1, 0, 2),
    )
    requests, query_heads, head_dim = queries.shape
    rotated = rotate_keys(projected[:, :, :head_dim], lengths)
    new_kv = jnp.concatenate([rotated, projected[:, :, head_dim:]], axis=-1).astype(jnp.bfloat16)
    pool_size, key_heads, page_len = (pool_keys.shape[0], pool_keys.shape[1], pool_keys.shape[2])
    group_size = query_heads // key_heads
    scaling = 1.0 / math.sqrt(head_dim)
    grouped = queries.reshape(requests, key_heads, group_size, head_dim)
    scores = (
        jnp.einsum("rgqd,pgtd->rgqpt", grouped, pool_keys, preferred_element_type=jnp.float32)
        * scaling
    )
    matches = page_table[:, :, None] == jnp.arange(pool_size, dtype=jnp.int32)[None, None, :]
    slot_of = jnp.sum(
        jnp.where(matches, jnp.arange(page_table.shape[1], dtype=jnp.int32)[None, :, None], 0),
        axis=1,
    )
    present = jnp.any(matches, axis=1)
    token_pos = (
        slot_of[:, :, None] * page_len + jnp.arange(page_len, dtype=jnp.int32)[None, None, :]
    )
    usable = (present[:, :, None] & (token_pos < lengths[:, None, None]))[:, None, None]
    masked = jnp.where(usable, scores, FLOOR_SCORE)
    local_high = jnp.max(masked, axis=-1)
    local_weights = jnp.where(usable, jnp.exp(masked - local_high[..., None]), 0.0)
    local_sums = jnp.sum(local_weights, axis=-1)
    local_out = jnp.einsum(
        "rgqpt,pgtd->rgqpd",
        local_weights.astype(jnp.bfloat16),
        pool_values,
        preferred_element_type=jnp.float32,
    )
    fresh_key = new_kv[:, :, :head_dim]
    fresh_value = new_kv[:, :, head_dim:].astype(jnp.float32)
    fresh_score = (
        jnp.einsum("rgqd,rgd->rgq", grouped, fresh_key, preferred_element_type=jnp.float32)
        * scaling
    )
    instances = lax.axis_size("inst")
    targets = move_target[:, 0]
    chosen = targets[None, :] == jnp.arange(instances, dtype=jnp.int32)[:, None]
    filled = jnp.any(chosen, axis=1)
    source_page = jnp.sum(jnp.where(chosen, move_page[None, :], 0), axis=1)
    label_out = jnp.where(filled, jnp.sum(jnp.where(chosen, move_request[None, :], 0), axis=1), -1)
    recv_keys, recv_values, labels_in = (
        lax.all_to_all(pool_keys[source_page], "inst", split_axis=0, concat_axis=0, tiled=True),
        lax.all_to_all(pool_values[source_page], "inst", split_axis=0, concat_axis=0, tiled=True),
        lax.all_to_all(label_out, "inst", split_axis=0, concat_axis=0, tiled=True),
    )
    asked_rows = grouped[jnp.maximum(labels_in, 0)]
    moved_high, moved_sums, moved_out = page_blocks(asked_rows, recv_keys, recv_values, scaling)
    valid_in = labels_in >= 0
    owners = labels_in[None, :] == jnp.arange(requests, dtype=jnp.int32)[:, None]
    moved_best = jnp.max(jnp.where(owners[:, :, None, None], moved_high[None], FLOOR_SCORE), axis=1)
    row_best = jnp.maximum(jnp.maximum(jnp.max(local_high, axis=-1), fresh_score), moved_best)
    local_factor = jnp.exp(local_high - row_best[..., None])
    fresh_factor = jnp.exp(fresh_score - row_best)
    moved_factor = jnp.where(
        valid_in[:, None, None], jnp.exp(moved_high - row_best[jnp.maximum(labels_in, 0)]), 0.0
    )
    owner_matrix = owners.astype(jnp.float32)
    denominator = (
        jnp.sum(local_factor * local_sums, axis=-1)
        + fresh_factor
        + jnp.einsum(
            "rn,ngq->rgq", owner_matrix, moved_factor * moved_sums, precision=lax.Precision.HIGHEST
        )
    )
    numerator = (
        jnp.sum(local_factor[..., None] * local_out, axis=3)
        + fresh_factor[..., None] * fresh_value[:, :, None, :]
    )
    numerator = numerator + jnp.einsum(
        "rn,ngqd->rgqd",
        owner_matrix,
        moved_factor[..., None] * moved_out,
        precision=lax.Precision.HIGHEST,
    )
    attention_out = (
        (numerator / denominator[..., None])
        .astype(jnp.bfloat16)
        .reshape(requests, query_heads * head_dim)
    )
    return (attention_out, new_kv)


def solution(mesh):
    return jax.shard_map(
        body,
        mesh=mesh,
        in_specs=(
            P("inst", "tp"),
            P("tp"),
            P("tp", None, None),
            P("inst", "tp", None),
            P("inst", "tp", None, None),
            P("inst", "tp", None, None),
            P("inst", None),
            P("inst"),
            P("inst", None),
            P("inst"),
            P("inst"),
        ),
        out_specs=(P("inst", "tp"), P("inst", "tp", None)),
        check_vma=False,
    )
```

profile of v0, /device:TPU:15, one launch (start us, length us, event | category | flops | bytes accessed | tf_op | source)
XLA Modules:
  0.0 166.2 jit_solution(2843879661034353648)
XLA Ops:
  7.2 0.9 fusion.45
  8.1 0.8 select_reduce_fusion.3
  8.9 0.7 copy.91
  9.5 6.6 %all-to-all-start = ((s32[16,1,1]{2,1,0:T(1,128)}), s32[16,1,1]{2,1,0:T(1,128)S(1)}, u32[]{:S(2)}, u32[]{:S(2)}) async-start(s32[16,1,1]{2,1,0:T(1,128)} %copy.91), calls=%async_computation.1 | async-start | bytes 16384 | tf_op jit(solution)/shard_map/all_to_all | solution.py:123
  16.1 0.0 reduce-scatter.2.cloned.1.call-start
  16.1 1.4 fusion.19
  17.5 3.8 %psum.7 = f32[128]{0:T(128)S(1)} all-reduce(f32[128]{0:T(128)S(1)} %fusion.19), channel_id=1, replica_groups=mesh['inst'=16,'tp'=2] {'tp'}, use_global_device_ids=true, to_apply=%region_5.6 | all-reduce | flops 128 | bytes 1024 | tf_op jit(solution)/shard_map/psum | solution.py:62
  21.3 0.7 convert_element_type.27
  22.0 8.1 %fusion.22 = f32[8,128,256]{2,1,0:T(8,128)} fusion(bf16[3072,8,256]{2,1,0:T(8,128)(2,1)} %param.13, bf16[128,3072]{1,0:T(8,128)(2,1)} %param.11, f32[3072]{0:T(1024)S(1)} %convert_element_type.27, f32[128]{0:T(128)S(1)} %add_rsqrt_fusion), kind=kOutput, calls=%fused_computation.29 | convolution fusion | flops 1612185600 | bytes 14430720 | tf_op jit(solution)/shard_map/rf,fgc->grc/dot_general | solution.py:70
  30.3 0.2 copy.88
  30.4 0.3 copy-done.14
  30.8 0.3 fusion.25
  31.0 13.1 %fusion.4 = (f32[128,4,6,20]{0,2,3,1:T(8,128)S(1)}, f32[4,20,128,128,6]{3,2,4,1,0:T(8,128)}) fusion(pred[128,20,128]{0,2,1:T(8,128)(4,1)S(1)} %fusion.25, bf16[128,4,6,128,1]{3,0,2,4,1:T(8,128)(2,1)S(1)} %bitcast.64, bf16[20,4,128,128]{3,2,1,0:T(8,128)(2,1)S(1)} %copy-done), kind=kOutput, calls=%fused_computation.11 | convolution fusion | flops 2036797440 | bytes 35438592 | tf_op jit(solution)/shard_map/rgqd,pgtd->rgqpt/dot_general | solution.py:85
  44.1 2.1 %gather_fusion.1 = bf16[16,4,128,128]{3,2,1,0:T(8,128)(2,1)} fusion(bf16[20,4,128,128]{3,2,1,0:T(8,128)(2,1)S(1)} %copy-done, s32[1024]{0:T(1024)S(1)} %pad_clamp_fusion), kind=kCustom, calls=%fused_computation.1 | custom fusion | bytes 4194368 | tf_op jit(solution)/shard_map/gather | solution.py:121
  46.2 7.2 %all-to-all-start.1 = ((bf16[16,4,128,128]{3,2,1,0:T(8,128)(2,1)}), bf16[16,4,128,128]{3,2,1,0:T(8,128)(2,1)S(1)}, u32[]{:S(2)}, u32[]{:S(2)}) async-start(bf16[16,4,128,128]{3,2,1,0:T(8,128)(2,1)} %gather_fusion.1), calls=%async_computation.2 | async-start | bytes 4194304 | tf_op jit(solution)/shard_map/all_to_all | solution.py:121
  53.4 0.9 multiply_cosine_fusion
  54.3 2.6 %copy.92 = bf16[128,4,6,128]{3,1,2,0:T(4,128)(2,1)} copy(bf16[128,4,6,128]{3,0,2,1:T(8,128)(2,1)} %bitcast.65) | data formatting | bytes 1572864 | tf_op jit(solution)/shard_map/reshape | solution.py:83
  57.0 3.9 %gather_fusion.3 = bf16[16,4,128,128]{3,2,1,0:T(8,128)(2,1)} fusion(bf16[20,4,128,128]{3,2,1,0:T(8,128)(2,1)} %param.16, s32[1024]{0:T(1024)S(1)} %pad_clamp_fusion), kind=kCustom, calls=%fused_computation.3 | custom fusion | bytes 4194368 | tf_op jit(solution)/shard_map/gather | solution.py:122
  60.9 15.1 %fusion.1 = (f32[128,4,6,20]{0,2,3,1:T(8,128)S(1)}, f32[128,4,6]{0,2,1:T(8,128)S(1)}) fusion(f32[4,20,128,128,6]{3,2,4,1,0:T(8,128)} %get-tuple-element.31, f32[128,4,6,20]{0,2,3,1:T(8,128)S(1)} %get-tuple-element.30, pred[128,20,128]{0,2,1:T(8,128)(4,1)S(1)} %fusion.25), kind=kLoop, calls=%fused_computation.8 | loop fusion | flops 47121408 | bytes 32288768 | tf_op jit(solution)/shard_map/reduce_sum | solution.py:101
  76.0 0.7 fusion.50
  76.7 2.4 %gather_fusion = bf16[16,4,6,128]{3,1,2,0:T(4,128)(2,1)} fusion(bf16[128,4,6,128]{3,1,2,0:T(4,128)(2,1)} %copy.92, s32[1024]{0:T(1024)S(1)} %pad_clamp_fusion.1), kind=kCustom, calls=%fused_computation | custom fusion | bytes 196672 | tf_op jit(solution)/shard_map/gather | solution.py:125
  79.1 0.9 compare_reduce_fusion
  80.0 0.6 iota_compare_fusion.1
  80.6 1.0 slice.35
  81.6 0.8 copy.97
  82.4 1.2 subtract_convert_fusion
  83.6 0.1 maximum_bitcast_fusion
  83.7 2.6 %fusion.26 = f32[128,4,1,6]{3,2,1,0:T(1,128)} fusion(bf16[128,4,6,128]{3,0,2,1:T(8,128)(2,1)} %bitcast.66, bf16[128,4,128,1]{2,0,1,3:T(8,128)(2,1)S(1)} %maximum_bitcast_fusion), kind=kOutput, calls=%fused_computation.35 | convolution fusion | flops 786432 | bytes 929792 | tf_op jit(solution)/shard_map/rgqd,rgd->rgq/dot_general | solution.py:111
  86.3 14.5 %all-to-all-done.1 = bf16[16,4,128,128]{3,2,1,0:T(8,128)(2,1)S(1)} async-done(((bf16[16,4,128,128]{3,2,1,0:T(8,128)(2,1)}), bf16[16,4,128,128]{3,2,1,0:T(8,128)(2,1)S(1)}, u32[]{:S(2)}, u32[]{:S(2)}) %all-to-all-start.1) | async-done | bytes 2097184 | tf_op jit(solution)/shard_map/all_to_all | solution.py:121
  100.8 4.9 %all-to-all-start.2 = ((bf16[16,4,128,128]{3,2,1,0:T(8,128)(2,1)}), bf16[16,4,128,128]{3,2,1,0:T(8,128)(2,1)}, u32[]{:S(2)}, u32[]{:S(2)}) async-start(bf16[16,4,128,128]{3,2,1,0:T(8,128)(2,1)} %gather_fusion.3), calls=%async_computation.3 | async-start | bytes 4194304 | tf_op jit(solution)/shard_map/all_to_all | solution.py:122
  105.7 0.1 pad_maximum_fusion
  105.9 0.9 copy.103
  106.8 1.0 copy.108
  107.8 2.2 %fusion.52 = (f32[16,4,6]{2,1,0:T(4,128)S(1)}, f32[16,4,6,128]{3,2,1,0:T(8,128)S(1)}) fusion(bf16[16,4,128,128]{3,2,1,0:T(8,128)(2,1)S(1)} %all-to-all-done.1, bf16[16,4,6,128]{3,1,2,0:T(4,128)(2,1)} %gather_fusion), kind=kOutput, calls=%fused_computation.89 | convolution fusion | flops 12680832 | bytes 2393600 | tf_op jit(solution)/shard_map/ngqd,ngtd->ngqt/dot_general | solution.py:33
  110.0 0.1 copy.94
  110.1 0.1 select_reduce_fusion
  110.3 0.2 copy.99
  110.5 0.1 multiply_reduce_fusion
  110.6 19.4 %fusion = f32[128,4,6,128]{3,0,2,1:T(8,128)S(1)} fusion(f32[128,4,6,20]{0,2,3,1:T(8,128)S(1)} %get-tuple-element.23, f32[4,20,128,128,6]{3,2,4,1,0:T(8,128)} %get-tuple-element.31, f32[128,4,6,20]{0,2,3,1:T(8,128)S(1)} %get-tuple-element.30, pred[128,20,128]{0,2,1:T(8,128)(4,1)S(1)} %fusion.25, bf16[20,4,128,128]{3,2,1,0:T(8,128)(2,1)} %param.16), kind=kOutput, calls=%fused_computation.5 | convolution fusion | flops 2067922944 | bytes 36470784 | tf_op jit(solution)/shard_map/rgqpt,pgtd->rgqpd/dot_general | solution.py:102
  130.0 1.6 copy.98
  131.6 0.7 gather_fusion.2
  132.3 0.3 fusion.33
  132.6 0.1 fusion.51
  132.8 0.8 convolution_add_fusion
  133.6 19.7 %all-to-all-done.2 = bf16[16,4,128,128]{3,2,1,0:T(8,128)(2,1)} async-done(((bf16[16,4,128,128]{3,2,1,0:T(8,128)(2,1)}), bf16[16,4,128,128]{3,2,1,0:T(8,128)(2,1)}, u32[]{:S(2)}, u32[]{:S(2)}) %all-to-all-start.2) | async-done | bytes 2097184 | tf_op jit(solution)/shard_map/all_to_all | solution.py:122
  153.3 2.5 %convolution_multiply_fusion = f32[16,4,6,128]{3,2,1,0:T(8,128)S(1)} fusion(bf16[16,4,128,128]{3,2,1,0:T(8,128)(2,1)} %all-to-all-done.2, f32[16,4,6,128]{3,2,1,0:T(8,128)S(1)} %get-tuple-element.33, f32[16,4,6]{2,1,0:T(4,128)} %copy-done.5, f32[16,4,6]{2,1,0:T(4,128)S(1)} %get-tuple-element.25), kind=kOutput, calls=%fused_computation.32 | convolution fusion | flops 12730368 | bytes 2493440 | tf_op jit(solution)/shard_map/ngqt,ngtd->ngqd/dot_general | solution.py:39
  155.7 2.4 %divide_convert_fusion = bf16[128,4,6,128]{0,3,2,1:T(8,128)(2,1)S(1)} fusion(f32[128,4,6,128]{0,3,2,1:T(8,128)S(1)} %copy-done.3, f32[128,4,6]{0,2,1:T(8,128)S(1)} %copy-done.15, f32[128,4,128]{0,2,1:T(8,128)} %copy.97, f32[128,4,6]{0,2,1:T(8,128)S(1)} %copy-done.8, f32[16,4,6,128]{3,2,1,0:T(8,128)S(1)} %convolution_multiply_fusion, s32[16]{0:T(128)} %copy-done.12), kind=kOutput, calls=%fused_computation.28 | convolution fusion | flops 77465600 | bytes 2842688 | tf_op jit(solution)/shard_map/rn,ngqd->rgqd/dot_general | solution.py:148
  158.1 1.2 copy.102
  (45 shorter events, 0.2 us)
Async XLA Ops:
  7.2 23.9 %copy-start = (bf16[20,4,128,128]{3,2,1,0:T(8,128)(2,1)S(1)}, bf16[20,4,128,128]{3,2,1,0:T(8,128)(2,1)}, u32[]{:S(2)}) copy-start(bf16[20,4,128,128]{3,2,1,0:T(8,128)(2,1)} %param.15) | copy-start | bytes 7864324
  9.5 36.7 %all-to-all-start = ((s32[16,1,1]{2,1,0:T(1,128)}), s32[16,1,1]{2,1,0:T(1,128)S(1)}, u32[]{:S(2)}, u32[]{:S(2)}) async-start(s32[16,1,1]{2,1,0:T(1,128)} %copy.91), calls=%async_computation.1 | async-start | bytes 16384 | tf_op jit(solution)/shard_map/all_to_all | solution.py:123
  16.1 64.5 %reduce-scatter.2.cloned.1.call-start = ((), (), s32[]{:S(2)}) async-start(), calls=%async_computation.4 | async-start | bytes 1572864 | tf_op jit(solution)/shard_map/reduce_scatter | solution.py:69
  22.0 8.1 %copy-start.6 = (s32[128,12]{0,1:T(8,128)S(1)}, s32[128,12]{0,1:T(8,128)}, u32[]{:S(2)}) copy-start(s32[128,12]{0,1:T(8,128)} %param.17) | copy-start | bytes 18436
  22.0 8.2 %copy-start.4 = (bf16[128,24,128]{2,1,0:T(8,128)(2,1)S(1)}, bf16[128,24,128]{2,1,0:T(8,128)(2,1)}, u32[]{:S(2)}) copy-start(bf16[128,24,128]{2,1,0:T(8,128)(2,1)} %param.14) | copy-start | bytes 2359300
  30.1 0.7 copy-start.14
  30.8 13.3 %copy-start.2 = (bf16[128,24,128]{2,0,1:T(8,128)(2,1)}, bf16[128,24,128]{2,0,1:T(8,128)(2,1)S(1)}, u32[]{:S(2)}) copy-start(bf16[128,24,128]{2,0,1:T(8,128)(2,1)S(1)} %copy.88) | copy-start | bytes 2359300
  46.2 54.6 %all-to-all-start.1 = ((bf16[16,4,128,128]{3,2,1,0:T(8,128)(2,1)}), bf16[16,4,128,128]{3,2,1,0:T(8,128)(2,1)S(1)}, u32[]{:S(2)}, u32[]{:S(2)}) async-start(bf16[16,4,128,128]{3,2,1,0:T(8,128)(2,1)} %gather_fusion.1), calls=%async_computation.2 | async-start | bytes 4194304 | tf_op jit(solution)/shard_map/all_to_all | solution.py:121
  76.7 4.0 %copy-start.12 = (s32[16]{0:T(128)}, s32[16]{0:T(128)S(1)}, u32[]{:S(2)}) copy-start(s32[16]{0:T(128)S(1)} %get-tuple-element.16) | copy-start | bytes 196
  76.7 4.0 %copy-start.10 = (s32[1024]{0:T(1024)}, s32[1024]{0:T(1024)S(1)}, u32[]{:S(2)}) copy-start(s32[1024]{0:T(1024)S(1)} %pad_clamp_fusion.1) | copy-start | bytes 12292
  100.8 52.4 %all-to-all-start.2 = ((bf16[16,4,128,128]{3,2,1,0:T(8,128)(2,1)}), bf16[16,4,128,128]{3,2,1,0:T(8,128)(2,1)}, u32[]{:S(2)}, u32[]{:S(2)}) async-start(bf16[16,4,128,128]{3,2,1,0:T(8,128)(2,1)} %gather_fusion.3), calls=%async_computation.3 | async-start | bytes 4194304 | tf_op jit(solution)/shard_map/all_to_all | solution.py:122
  105.7 4.4 %copy-start.9 = (pred[128,16]{0,1:T(8,128)(4,1)S(1)}, pred[128,16]{0,1:T(8,128)(4,1)}, u32[]{:S(2)}) copy-start(pred[128,16]{0,1:T(8,128)(4,1)} %iota_compare_fusion.1) | copy-start | bytes 6148
  110.0 22.6 %copy-start.5 = (f32[16,4,6]{2,1,0:T(4,128)}, f32[16,4,6]{2,1,0:T(4,128)S(1)}, u32[]{:S(2)}) copy-start(f32[16,4,6]{2,1,0:T(4,128)S(1)} %get-tuple-element.32) | copy-start | bytes 4612
  110.3 22.4 %copy-start.7 = (f32[128,4,6]{0,2,1:T(8,128)}, f32[128,4,6]{0,2,1:T(8,128)S(1)}, u32[]{:S(2)}) copy-start(f32[128,4,6]{0,2,1:T(8,128)S(1)} %get-tuple-element.20) | copy-start | bytes 36868
  130.0 2.7 %copy-start.11 = (pred[16]{0:T(512)(128)(4,1)S(1)}, pred[16]{0:T(512)(128)(4,1)}, u32[]{:S(2)}) copy-start(pred[16]{0:T(512)(128)(4,1)} %compare_reduce_fusion) | copy-start | bytes 52
  130.0 2.8 %copy-start.13 = (s32[16]{0:T(128)S(1)}, s32[16]{0:T(128)}, u32[]{:S(2)}) copy-start(s32[16]{0:T(128)} %copy-done.12) | copy-start | bytes 196
  133.6 22.2 %copy-start.8 = (f32[128,4,6]{0,2,1:T(8,128)S(1)}, f32[128,4,6]{0,2,1:T(8,128)}, u32[]{:S(2)}) copy-start(f32[128,4,6]{0,2,1:T(8,128)} %copy-done.7) | copy-start | bytes 36868
  153.2 2.5 %copy-start.3 = (f32[128,4,6,128]{0,3,2,1:T(8,128)S(1)}, f32[128,4,6,128]{0,3,2,1:T(8,128)}, u32[]{:S(2)}) copy-start(f32[128,4,6,128]{0,3,2,1:T(8,128)} %copy.98) | copy-start | bytes 4718596
  153.3 2.5 %copy-start.15 = (f32[128,4,6]{0,2,1:T(8,128)S(1)}, f32[128,4,6]{0,2,1:T(8,128)}, u32[]{:S(2)}) copy-start(f32[128,4,6]{0,2,1:T(8,128)} %convolution_add_fusion) | copy-start | bytes 36868
  153.3 6.1 %copy-start.1 = (bf16[20,4,128,128]{3,2,1,0:T(8,128)(2,1)S(1)}, bf16[20,4,128,128]{3,2,1,0:T(8,128)(2,1)}, u32[]{:S(2)}) copy-start(bf16[20,4,128,128]{3,2,1,0:T(8,128)(2,1)} %param.15) | copy-start | bytes 7864324
Sparse Core Ops, SparseCore 0:
  30.2 21.0 reduce-scatter.1
where the time goes:
time: 167 us; the launch traced here: 166 us
  matrix products  51 us (31%)
  waiting for transfers between devices  34.2 us (20%)
  other arithmetic  24.4 us (15%)
  local copies, waits for them, and re-layouts  19.8 us (12%)
  starting transfers between devices  18.7 us (11%)
  between operations  14.3 us (9%)
  blocking collectives  3.79 us (2%)
    all_to_all x1, waiting for transfers between devices, body(): lax.all_to_all(pool_values[source_page], 'inst', split_axis=0, concat_axi...  19.7 us
    dot_general x1, matrix products, body(): jnp.einsum('rgqpt,pgtd->rgqpd', local_weights.astype(jnp.bfloat16), pool_...  19.4 us
    reduce_sum x1, other arithmetic, body(): local_sums = jnp.sum(local_weights, axis=-1)  15.1 us
    all_to_all x1, waiting for transfers between devices, body(): lax.all_to_all(pool_keys[source_page], 'inst', split_axis=0, concat_axis=...  14.5 us
    dot_general x1, matrix products, body(): jnp.einsum('rgqd,pgtd->rgqpt', grouped, pool_keys, preferred_element_type...  13.1 us
    dot_general x1, matrix products, body(): jnp.einsum('rf,fgc->grc', normed, kv_weight, preferred_element_type=jnp.f...  8.08 us
    all_to_all x1, starting transfers between devices, body(): lax.all_to_all(pool_keys[source_page], 'inst', split_axis=0, concat_axis=...  7.16 us
    all_to_all x1, starting transfers between devices, body(): lax.all_to_all(label_out, 'inst', split_axis=0, concat_axis=0, tiled=True)  6.55 us
  transfers between devices with their start and end apart: 4, of which 2 were waited for; matrix products, arithmetic and copies ran while one was open for 52% of the time, Pallas kernels for 0%

commit v1 on v0

v1 whole, which is shorter than its diff:
```python
import functools
import math

import jax
import jax.numpy as jnp
from jax import lax
from jax.experimental import pallas as pl
from jax.experimental.pallas import tpu as pltpu
from jax.sharding import PartitionSpec as P

EPSILON = 1e-05
ROPE_BASE = 1000000.0
MASKED = -1e30
LOWEST = -1e20
LOG2E = math.log2(math.e)
MESH = pl.DeviceIdType.MESH
VMEM_BYTES = 56 * 1024 * 1024
F32 = jnp.float32
BF16 = jnp.bfloat16


def greet(axes):
    barrier = pltpu.get_barrier_semaphore()
    total = 0
    for axis in axes:
        size = lax.axis_size(axis)
        me = lax.axis_index(axis)

        def signal(k, carry, axis=axis, size=size, me=me):
            pl.semaphore_signal(
                barrier, inc=1, device_id={axis: lax.rem(me + k, size)}, device_id_type=MESH
            )
            return carry

        lax.fori_loop(1, size, signal, 0)
        total += size - 1
    pl.semaphore_wait(barrier, total)


def exchange(axis, source_of, landing, send, recv):
    size = lax.axis_size(axis)
    me = lax.axis_index(axis)

    def copy(k):
        peer = lax.rem(me + k, size)
        return pltpu.make_async_remote_copy(
            src_ref=source_of(peer),
            dst_ref=landing.at[me],
            send_sem=send.at[k],
            recv_sem=recv.at[k],
            device_id={axis: peer},
            device_id_type=MESH,
        )

    def arrival(k):
        peer = lax.rem(me + size - k, size)
        return pltpu.make_async_remote_copy(
            src_ref=source_of(peer),
            dst_ref=landing.at[peer],
            send_sem=send.at[k],
            recv_sem=recv.at[k],
            device_id={axis: peer},
            device_id_type=MESH,
        )

    def start():
        def step(k, carry):
            copy(k).start()
            return carry

        lax.fori_loop(1, size, step, 0)

    def wait():
        def step(k, carry):
            arrival(k).wait_recv()
            copy(k).wait_send()
            return carry

        lax.fori_loop(1, size, step, 0)

    return start, wait


def ask_kernel(
    heads, group, plan_ref, sq_ref, q_ref, qx_ref, lab_ref, sqsum_ref,
    plans, sqs, stage, asked, landed, sems_plan, sems_sq, sems_q,
):
    ni = lax.axis_size("inst")
    me = lax.axis_index("inst")
    me_tp = lax.axis_index("tp")
    greet(("inst", "tp"))
    start_plan, wait_plan = exchange("inst", lambda p: plan_ref, plans, sems_plan.at[0], sems_plan.at[1])
    start_sq, wait_sq = exchange("tp", lambda p: sq_ref, sqs, sems_sq.at[0], sems_sq.at[1])
    start_plan()
    start_sq()
    plans[me] = plan_ref[...]
    sqs[me_tp] = sq_ref[...]
    stage[...] = jnp.zeros_like(stage)
    wait_plan()
    mine = plans[:, 0, :] == me.astype(F32)
    label = jnp.sum(jnp.where(mine, plans[:, 1, :] + 1.0, 0.0), axis=1, keepdims=True) - 1.0
    lanes = lax.broadcasted_iota(jnp.int32, (ni, q_ref.shape[1]), 1).astype(F32)
    lab_ref[...] = jnp.broadcast_to(label, lab_ref.shape)
    pick = jnp.where(label == lanes, 1.0, 0.0).astype(BF16)
    for h in range(heads):
        stage[:, h, :] = jnp.dot(pick, q_ref[h], preferred_element_type=F32)
    asked[...] = stage[...].astype(BF16)
    start_q, wait_q = exchange("inst", lambda p: asked.at[p], landed, sems_q.at[0], sems_q.at[1])
    start_q()
    landed[me] = asked[me]
    wait_sq()
    sqsum_ref[...] = jnp.sum(sqs[...], axis=0)
    wait_q()
    stage[...] = landed[...].astype(F32)
    qx_ref[...] = jnp.zeros_like(qx_ref)
    for g in range(heads // group):
        for q in range(group):
            qx_ref[g, q * ni : (q + 1) * ni, :] = stage[:, g * group + q, :].astype(BF16)


def attend_kernel(
    ni, target_ref, page_ref, q_ref, qx_ref, k_ref, v_ref, pt_ref, len_ref,
    o_ref, ml_ref, vb_ref, sg_ref, lim, limx, vt, s_buf, sx_buf,
):
    pool, page, hd = k_ref.shape[0], k_ref.shape[2], k_ref.shape[3]
    group = q_ref.shape[0]
    nx = qx_ref.shape[1]
    scale = LOG2E / math.sqrt(hd)

    @pl.when(pl.program_id(0) == 0)
    def _():
        slots = pt_ref.shape[0]
        first = lax.broadcasted_iota(jnp.int32, pt_ref.shape, 0) * page
        room = jnp.clip(len_ref[...] - first, 0, page).astype(F32)
        column = lax.broadcasted_iota(jnp.int32, (1, nx), 1)
        owner = lax.rem(column, ni)
        wanted = jnp.full((1, nx), -1, jnp.int32)
        for m in range(target_ref.shape[0]):
            wanted = jnp.where(owner == target_ref[m], page_ref[m], wanted)
        wanted = jnp.where(column < group * ni, wanted, -1)
        for p in range(pool):
            lim[p : p + 1, :] = jnp.sum(
                jnp.where(pt_ref[...] == p, room, 0.0), axis=0, keepdims=True
            )
            limx[p : p + 1, :] = jnp.where(wanted == p, float(page), 0.0)
        vt[hd:, :] = jnp.ones((vt.shape[0] - hd, vt.shape[1]), BF16)

    for p in range(pool):
        vt[:hd, p * page : (p + 1) * page] = v_ref[p, 0].T
    pages = 4 if pool % 4 == 0 else 1
    span = pages * page
    chunks = pool // pages
    tokens = lax.broadcasted_iota(jnp.int32, (page, 128), 0).astype(F32)
    pair = 2 if group % 2 == 0 else 1
    tiles = [("main", j) for j in range(group // pair)] + [("extra", j) for j in range(nx // 128)]
    state = {}

    def first_pass(i, ci):
        kind, j = tiles[i]
        if kind == "main":
            qs = q_ref[j * pair : (j + 1) * pair].reshape(pair * 128, hd)
        else:
            qs = qx_ref[0, j * 128 : (j + 1) * 128, :]
        width = qs.shape[0]
        keys = k_ref[ci * pages : (ci + 1) * pages, 0].reshape(span, hd)
        s = lax.dot_general(keys, qs, (((1,), (1,)), ((), ())), preferred_element_type=F32)
        highs = state.get(i)
        if highs is None:
            highs = [jnp.full((8, 128), LOWEST, F32) for _ in range(width // 128)]
        for pp in range(pages):
            p = ci * pages + pp
            if kind == "main":
                usable = tokens < lim[p : p + 1, :]
            else:
                usable = tokens < limx[p : p + 1, j * 128 : (j + 1) * 128]
            for w in range(width // 128):
                part = jnp.where(
                    usable, s[pp * page : (pp + 1) * page, w * 128 : (w + 1) * 128], MASKED
                )
                s_buf[i % 2, p * page : (p + 1) * page, w * 128 : (w + 1) * 128] = part
                highs[w] = jnp.maximum(highs[w], jnp.max(part.reshape(page // 8, 8, 128), axis=0))
        state[i] = highs

    def second_pass(i, ci, tops, total):
        width = tops.shape[1]
        rows = slice(ci * span, (ci + 1) * span)
        weights = jnp.exp2(s_buf[i % 2, rows, :width] * scale - tops).astype(BF16)
        part = jnp.dot(vt[:, rows], weights, preferred_element_type=F32)
        return part if total is None else total + part

    for ci in range(chunks):
        first_pass(0, ci)
    for i, (kind, j) in enumerate(tiles):
        tops = jnp.concatenate(
            [jnp.max(high, axis=0, keepdims=True) for high in state[i]], axis=1
        ) * scale
        total = None
        for ci in range(chunks):
            if i + 1 < len(tiles):
                first_pass(i + 1, ci)
            total = second_pass(i, ci, tops, total)
        sums = total[hd : hd + 1, :]
        if kind == "main":
            columns = slice(j * pair * 128, (j + 1) * pair * 128)
            o_ref[0, :, columns] = total[:hd]
            ml_ref[0, 0:1, columns] = tops
            ml_ref[0, 1:2, columns] = sums
        else:
            columns = slice(j * 128, (j + 1) * 128)
            safe = jnp.maximum(sums, 1e-30)
            vb_ref[0, columns, :] = (total[:hd] / safe).T
            sg_ref[0, :, columns] = jnp.broadcast_to(tops + jnp.log(safe) * LOG2E, (8, 128))


def answer_kernel(
    heads, group, vb_ref, sg_ref, vin_ref, sin_ref,
    stage, told, table, landed, tables, sems_v, sems_s,
):
    ni = lax.axis_size("inst")
    me = lax.axis_index("inst")
    stage[...] = jnp.zeros_like(stage)
    table[...] = jnp.zeros_like(table)
    for g in range(heads // group):
        table[g : g + 1, :] = sg_ref[g, 0:1, :]
        for q in range(group):
            stage[:, g * group + q, :] = vb_ref[g, q * ni : (q + 1) * ni, :]
    told[...] = stage[...].astype(BF16)
    greet(("inst",))
    start_v, wait_v = exchange("inst", lambda p: told.at[p], landed, sems_v.at[0], sems_v.at[1])
    start_s, wait_s = exchange("inst", lambda p: table, tables, sems_s.at[0], sems_s.at[1])
    start_v()
    start_s()
    landed[me] = told[me]
    tables[me] = table[...]
    wait_v()
    wait_s()
    vin_ref[...] = landed[...].astype(F32)
    sin_ref[...] = tables[...]


def join_kernel(
    features, group, heads, me_ref, vin_ref, sin_ref, lab_ref, o_ref, ml_ref, q_ref, proj_ref,
    sq_ref, len_ref, out_ref, kv_ref,
):
    ni, nx = sin_ref.shape[0], sin_ref.shape[2]
    hd = q_ref.shape[2]
    req = q_ref.shape[1]
    half = hd // 2
    scale = LOG2E / math.sqrt(hd)
    me = me_ref[0]
    inverse = jnp.broadcast_to(lax.rsqrt(sq_ref[0:1, :] / features + EPSILON), (hd, req)).T
    lane = lax.broadcasted_iota(jnp.int32, (1, hd), 1)
    step = lax.rem(lane, half).astype(F32)
    frequency = jnp.exp(step * (-2.0 / hd * math.log(ROPE_BASE)))
    angles = jnp.broadcast_to(len_ref[...].astype(F32), (hd, req)).T * frequency
    cosine = jnp.cos(angles)
    sine = jnp.sin(angles) * jnp.where(lane < half, -1.0, 1.0)
    lanes = lax.broadcasted_iota(jnp.int32, (ni, req), 1).astype(F32)
    owned = lab_ref[...] == lanes
    columns = lax.broadcasted_iota(jnp.int32, (ni, nx), 1)
    ones = jnp.ones((8, hd), F32)
    for g in range(heads // group):
        x = proj_ref[g, :, :hd] * inverse
        rotated = (x * cosine + pltpu.roll(x, half, 1) * sine).astype(BF16)
        value = (proj_ref[g, :, hd:] * inverse).astype(BF16)
        kv_ref[:, 2 * g * hd : (2 * g + 1) * hd] = rotated
        kv_ref[:, (2 * g + 1) * hd : (2 * g + 2) * hd] = value
        key = rotated.astype(F32)
        value_t = value.astype(F32).T
        for q in range(group):
            h = g * group + q
            tile = slice(q * req, (q + 1) * req)
            fresh = lax.dot_general(
                ones, q_ref[h].astype(F32) * key, (((1,), (1,)), ((), ())),
                precision=lax.Precision.HIGHEST, preferred_element_type=F32,
            )[0:1] * scale
            level = jnp.sum(
                jnp.where(columns == q * ni + me, sin_ref[:, g, :], 0.0), axis=1, keepdims=True
            )
            moved = jnp.where(owned, level, MASKED)
            top = ml_ref[g, 0:1, tile]
            best = jnp.maximum(jnp.maximum(top, fresh), jnp.max(moved, axis=0, keepdims=True))
            local_factor = jnp.exp2(top - best)
            fresh_factor = jnp.exp2(fresh - best)
            moved_factor = jnp.where(owned, jnp.exp2(moved - best), 0.0)
            bottom = (
                local_factor * ml_ref[g, 1:2, tile]
                + fresh_factor
                + jnp.sum(moved_factor, axis=0, keepdims=True)
            )
            top_sum = (
                o_ref[g, :, tile] * local_factor
                + value_t * fresh_factor
                + lax.dot_general(
                    vin_ref[:, h, :].astype(BF16), moved_factor.astype(BF16),
                    (((0,), (0,)), ((), ())), preferred_element_type=F32,
                )
            )
            out_ref[:, h * hd : (h + 1) * hd] = (top_sum / bottom).T.astype(BF16)


def body(
    hidden_state, norm_gain, kv_weight, queries, pool_keys, pool_values,
    page_table, lengths, move_target, move_page, move_request,
):
    ni, nt = lax.axis_size("inst"), lax.axis_size("tp")
    req, heads, hd = queries.shape
    pool, key_heads, page, _ = pool_keys.shape
    group = heads // key_heads
    moves = move_page.shape[0]
    features = hidden_state.shape[1] * nt
    padded = -(-heads // 16) * 16
    nx = -(-group * ni // 128) * 128
    params = functools.partial(pltpu.CompilerParams, vmem_limit_bytes=VMEM_BYTES)
    vmem = pl.BlockSpec(memory_space=pltpu.VMEM)
    smem = pl.BlockSpec(memory_space=pltpu.SMEM)

    widened = hidden_state.astype(F32)
    squares = jnp.sum(widened * widened, axis=1)
    scaled = (widened * norm_gain.astype(F32)[None, :]).astype(BF16)
    partial = jnp.einsum("rf,fgc->grc", scaled, kv_weight, preferred_element_type=F32)
    projected = lax.psum_scatter(partial, "tp", scatter_dimension=0, tiled=True)

    by_head = jnp.transpose(queries, (1, 0, 2))
    plan = jnp.pad(
        jnp.stack([move_target[:, 0], move_request]).astype(F32),
        ((0, 6), (0, 128 - moves)),
        constant_values=-1.0,
    )
    sq_tile = jnp.broadcast_to(squares[None, :], (8, req))
    qx, label, sq_total = pl.pallas_call(
        functools.partial(ask_kernel, heads, group),
        out_shape=(
            jax.ShapeDtypeStruct((key_heads, nx, hd), BF16),
            jax.ShapeDtypeStruct((ni, req), F32),
            jax.ShapeDtypeStruct((8, req), F32),
        ),
        in_specs=[vmem] * 3,
        out_specs=(vmem,) * 3,
        scratch_shapes=[
            pltpu.VMEM((ni, 8, 128), F32),
            pltpu.VMEM((nt, 8, req), F32),
            pltpu.VMEM((ni, padded, hd), F32),
            pltpu.VMEM((ni, padded, hd), BF16),
            pltpu.VMEM((ni, padded, hd), BF16),
            pltpu.SemaphoreType.DMA((2, ni)),
            pltpu.SemaphoreType.DMA((2, nt)),
            pltpu.SemaphoreType.DMA((2, ni)),
        ],
        compiler_params=params(collective_id=0, has_side_effects=True),
        name="ask",
    )(plan, sq_tile, by_head)

    tokens = pool * page
    work = 4 * heads * (req + ni) * tokens * hd
    local, levels, moved_mean, moved_level = pl.pallas_call(
        functools.partial(attend_kernel, ni),
        grid=(key_heads,),
        out_shape=(
            jax.ShapeDtypeStruct((key_heads, hd, group * req), F32),
            jax.ShapeDtypeStruct((key_heads, 8, group * req), F32),
            jax.ShapeDtypeStruct((key_heads, nx, hd), F32),
            jax.ShapeDtypeStruct((key_heads, 8, nx), F32),
        ),
        in_specs=[
            smem,
            smem,
            pl.BlockSpec((group, req, hd), lambda g: (g, 0, 0)),
            pl.BlockSpec((1, nx, hd), lambda g: (g, 0, 0)),
            pl.BlockSpec((pool, 1, page, hd), lambda g: (0, g, 0, 0)),
            pl.BlockSpec((pool, 1, page, hd), lambda g: (0, g, 0, 0)),
            pl.BlockSpec((page_table.shape[1], req), lambda g: (0, 0)),
            pl.BlockSpec((1, req), lambda g: (0, 0)),
        ],
        out_specs=(
            pl.BlockSpec((1, hd, group * req), lambda g: (g, 0, 0)),
            pl.BlockSpec((1, 8, group * req), lambda g: (g, 0, 0)),
            pl.BlockSpec((1, nx, hd), lambda g: (g, 0, 0)),
            pl.BlockSpec((1, 8, nx), lambda g: (g, 0, 0)),
        ),
        scratch_shapes=[
            pltpu.VMEM((pool, req), F32),
            pltpu.VMEM((pool, nx), F32),
            pltpu.VMEM((hd + 16, tokens), BF16),
            pltpu.VMEM((2, tokens, 256), F32),
            pltpu.VMEM((8, 128), F32),
        ],
        compiler_params=params(),
        cost_estimate=pl.CostEstimate(
            flops=work, bytes_accessed=4 * pool_keys.size, transcendentals=heads * req * tokens
        ),
        name="attend",
    )(
        move_target[:, 0], move_page, by_head, qx, pool_keys, pool_values,
        page_table.T, lengths[None, :],
    )

    moved_in, levels_in = pl.pallas_call(
        functools.partial(answer_kernel, heads, group),
        out_shape=(
            jax.ShapeDtypeStruct((ni, padded, hd), F32),
            jax.ShapeDtypeStruct((ni, 8, nx), F32),
        ),
        in_specs=[vmem] * 2,
        out_specs=(vmem,) * 2,
        scratch_shapes=[
            pltpu.VMEM((ni, padded, hd), F32),
            pltpu.VMEM((ni, padded, hd), BF16),
            pltpu.VMEM((8, nx), F32),
            pltpu.VMEM((ni, padded, hd), BF16),
            pltpu.VMEM((ni, 8, nx), F32),
            pltpu.SemaphoreType.DMA((2, ni)),
            pltpu.SemaphoreType.DMA((2, ni)),
        ],
        compiler_params=params(collective_id=1, has_side_effects=True),
        name="answer",
    )(moved_mean, moved_level)

    me = lax.axis_index("inst").astype(jnp.int32).reshape(1)
    attention_out, new_kv = pl.pallas_call(
        functools.partial(join_kernel, features, group, heads),
        out_shape=(
            jax.ShapeDtypeStruct((req, heads * hd), BF16),
            jax.ShapeDtypeStruct((req, key_heads * 2 * hd), BF16),
        ),
        in_specs=[smem] + [vmem] * 9,
        out_specs=(vmem,) * 2,
        compiler_params=params(),
        name="join",
    )(
        me, moved_in, levels_in, label, local, levels, by_head, projected, sq_total,
        lengths[None, :],
    )
    return (attention_out, new_kv.reshape(req, key_heads, 2 * hd))


def solution(mesh):
    return jax.shard_map(
        body,
        mesh=mesh,
        in_specs=(
            P("inst", "tp"),
            P("tp"),
            P("tp", None, None),
            P("inst", "tp", None),
            P("inst", "tp", None, None),
            P("inst", "tp", None, None),
            P("inst", None),
            P("inst"),
            P("inst", None),
            P("inst"),
            P("inst"),
        ),
        out_specs=(P("inst", "tp"), P("inst", "tp", None)),
        check_vma=False,
    )
```

time: 167 us -> 84.4 us (0.51)
  the two profiles are of different devices: /device:TPU:15 before, /device:TPU:0 now
where the time goes in v1:
time: 84.4 us; the launch traced here: 84.1 us
  Pallas kernels  57 us (68%)
  between operations  14.1 us (17%)
  matrix products  7.95 us (9%)
  local copies, waits for them, and re-layouts  4.12 us (5%)
  other arithmetic  0.94 us (1%)
    pallas_call x1, Pallas kernels, body(): pl.pallas_call(functools.partial(ask_kernel, heads, group), out_shape=(ja...  17.7 us
    pallas_call x1, Pallas kernels, body(): pl.pallas_call(functools.partial(attend_kernel, ni), grid=(key_heads,), o...  16.7 us
    pallas_call x1, Pallas kernels, body(): pl.pallas_call(functools.partial(join_kernel, features, group, heads), ou...  11.4 us
    pallas_call x1, Pallas kernels, body(): pl.pallas_call(functools.partial(answer_kernel, heads, group), out_shape=...  11.2 us
    dot_general x1, matrix products, body(): jnp.einsum('rf,fgc->grc', scaled, kv_weight, preferred_element_type=F32)  7.95 us
    reshape x1, local copies, waits for them, and re-layouts, body(): return (attention_out, new_kv.reshape(req, key_heads, 2 * hd))  1.84 us
  transfers between devices with their start and end apart: 1, of which 0 were waited for; matrix products, arithmetic and copies ran while one was open for 3% of the time, Pallas kernels for 54%

profile of v1, /device:TPU:0, one launch (start us, length us, event | category | flops | bytes accessed | tf_op | source)
XLA Modules:
  0.0 84.1 jit_solution(13165682918933328807)
XLA Ops:
  7.2 0.0 reduce-scatter.2.cloned.1.call-start
  7.2 0.7 convert_element_type.14
  7.9 0.0 copy-start.1
  7.9 7.9 %fusion.4 = f32[8,128,256]{2,1,0:T(8,128)} fusion(bf16[3072,8,256]{2,1,0:T(8,128)(2,1)} %param.13, bf16[128,3072]{1,0:T(8,128)(2,1)} %param.11, f32[3072]{0:T(1024)S(1)} %convert_element_type.14), kind=kOutput, calls=%fused_computation.6 | convolution fusion | flops 1611792384 | bytes 14430208 | tf_op jit(solution)/shard_map/rf,fgc->grc/dot_general | solution.py:321
  15.9 0.0 copy-start.2
  15.9 0.0 copy-start.3
  15.9 0.0 copy-start
  15.9 0.0 reduce-scatter.2.cloned.1.call-update
  15.9 0.0 copy-done.1
  15.9 1.1 %copy.20 = bf16[128,24,128]{2,0,1:T(8,128)(2,1)} copy(bf16[128,24,128]{2,1,0:T(8,128)(2,1)S(1)} %copy-done.1) | data formatting | bytes 1572864 | tf_op args[3]
  17.0 0.0 copy-done.2
  17.0 0.0 copy-done.3
  17.0 0.6 pad.4.plan_ref
  17.6 0.0 copy-done
  17.6 0.2 fusion.2
  17.8 0.6 broadcast_in_dim.4.sq_ref
  18.4 17.7 %ask.1 = (bf16[4,128,128]{2,1,0:T(8,128)(2,1)}, f32[16,128]{1,0:T(8,128)}, f32[8,128]{1,0:T(8,128)}) custom-call(f32[8,128]{1,0:T(8,128)} %pad.4.plan_ref, f32[8,128]{1,0:T(8,128)} %broadcast_in_dim.4.sq_ref, bf16[24,128,128]{2,1,0:T(8,128)(2,1)} %bitcast.14), custom_call_target="tpu_custom_call" | custom-call | tf_op jit(solution)/shard_map/ask/pallas_call | solution.py:331
  36.1 16.7 %attend.1 = (f32[4,128,768]{2,1,0:T(8,128)}, f32[4,8,768]{2,1,0:T(8,128)}, f32[4,128,128]{2,1,0:T(8,128)}, f32[4,8,128]{2,1,0:T(8,128)}) custom-call(s32[8]{0:T(128)} %bitcast.20, s32[8]{0:T(128)} %page_ref.1, bf16[24,128,128]{2,1,0:T(8,128)(2,1)} %bitcast.15, bf16[4,128,128]{2,1,0:T(8,128)(2,1)} %get-tuple-element.13.qx_ref, ...), custom_call_target="tpu_custom_call" | custom-call | flops 4529848320 | bytes 5242880 | tf_op jit(solution)/shard_map/attend/pallas_call | solution.py:356
  52.8 11.2 %answer.1 = (f32[16,32,128]{2,1,0:T(8,128)}, f32[16,8,128]{2,1,0:T(8,128)}) custom-call(f32[4,128,128]{2,1,0:T(8,128)} %get-tuple-element.14.vb_ref, f32[4,8,128]{2,1,0:T(8,128)} %get-tuple-element.15.sg_ref), custom_call_target="tpu_custom_call" | custom-call | tf_op jit(solution)/shard_map/answer/pallas_call | solution.py:398
  64.0 0.0 reduce-scatter.2.cloned.1.call-done.proj_ref
  64.0 11.4 %join.1 = (bf16[128,3072]{1,0:T(8,128)(2,1)}, bf16[128,1024]{1,0:T(8,128)(2,1)}) custom-call(s32[1]{0:T(128)} %bitcast.me_ref, f32[16,32,128]{2,1,0:T(8,128)} %get-tuple-element.16.vin_ref, f32[16,8,128]{2,1,0:T(8,128)} %get-tuple-element.17.sin_ref, f32[16,128]{1,0:T(8,128)} %get-tuple-element.18.lab_ref, f32[4,128,768]{2,1,0:T(8,128)} %get-tuple-element.19.o_ref, ...), custom_call_target="tpu_custom_call" | custom-call | tf_op jit(solution)/shard_map/join/pallas_call | solution.py:420
  75.4 1.8 %reshape.13 = bf16[128,4,256]{2,1,0:T(4,128)(2,1)} reshape(bf16[128,1024]{1,0:T(8,128)(2,1)} %get-tuple-element.23) | data formatting | bytes 524288 | tf_op jit(solution)/shard_map/reshape | solution.py:434
  (1 shorter events, 0.0 us)
Async XLA Ops:
  7.2 56.9 %reduce-scatter.2.cloned.1.call-start = ((), (), s32[]{:S(2)}) async-start(), calls=%async_computation.1 | async-start | bytes 1572864 | tf_op jit(solution)/shard_map/reduce_scatter | solution.py:322
  7.9 8.0 %copy-start.1 = (bf16[128,24,128]{2,1,0:T(8,128)(2,1)S(1)}, bf16[128,24,128]{2,1,0:T(8,128)(2,1)}, u32[]{:S(2)}) copy-start(bf16[128,24,128]{2,1,0:T(8,128)(2,1)} %param.14) | copy-start | bytes 2359300
  15.9 1.1 %copy-start.2 = (s32[8]{0:T(128)S(1)}, s32[8]{0:T(128)}, u32[]{:S(2)}) copy-start(s32[8]{0:T(128)} %param.21) | copy-start | bytes 100
  15.9 1.1 %copy-start.3 = (s32[8,1]{0,1:T(1,128)S(1)}, s32[8,1]{0,1:T(1,128)}, u32[]{:S(2)}) copy-start(s32[8,1]{0,1:T(1,128)} %param.19) | copy-start | bytes 100
  15.9 1.7 %copy-start = (bf16[128,3072]{1,0:T(8,128)(2,1)S(1)}, bf16[128,3072]{1,0:T(8,128)(2,1)}, u32[]{:S(2)}) copy-start(bf16[128,3072]{1,0:T(8,128)(2,1)} %param.11) | copy-start | bytes 2359300
Sparse Core Ops, SparseCore 0:
  16.0 23.0 reduce-scatter.1

commit v2 on v1

v2 whole, which is shorter than its diff:
```python
import functools
import math

import jax
import jax.numpy as jnp
from jax import lax
from jax.experimental import pallas as pl
from jax.experimental.pallas import tpu as pltpu
from jax.sharding import PartitionSpec as P

EPSILON = 1e-05
ROPE_BASE = 1000000.0
MASKED = -1e30
LOWEST = -1e20
LOG2E = math.log2(math.e)
MESH = pl.DeviceIdType.MESH
VMEM_BYTES = 56 * 1024 * 1024
F32 = jnp.float32
BF16 = jnp.bfloat16


def greet(axes):
    barrier = pltpu.get_barrier_semaphore()
    total = 0
    for axis in axes:
        size = lax.axis_size(axis)
        me = lax.axis_index(axis)

        def signal(k, carry, axis=axis, size=size, me=me):
            pl.semaphore_signal(
                barrier, inc=1, device_id={axis: lax.rem(me + k, size)}, device_id_type=MESH
            )
            return carry

        lax.fori_loop(1, size, signal, 0)
        total += size - 1
    pl.semaphore_wait(barrier, total)


def exchange(axis, source_of, landing, send, recv):
    size = lax.axis_size(axis)
    me = lax.axis_index(axis)

    def copy(k):
        peer = lax.rem(me + k, size)
        return pltpu.make_async_remote_copy(
            src_ref=source_of(peer),
            dst_ref=landing.at[me],
            send_sem=send.at[k],
            recv_sem=recv.at[k],
            device_id={axis: peer},
            device_id_type=MESH,
        )

    def arrival(k):
        peer = lax.rem(me + size - k, size)
        return pltpu.make_async_remote_copy(
            src_ref=source_of(peer),
            dst_ref=landing.at[peer],
            send_sem=send.at[k],
            recv_sem=recv.at[k],
            device_id={axis: peer},
            device_id_type=MESH,
        )

    def start():
        def step(k, carry):
            copy(k).start()
            return carry

        lax.fori_loop(1, size, step, 0)

    def wait():
        def step(k, carry):
            arrival(k).wait_recv()
            copy(k).wait_send()
            return carry

        lax.fori_loop(1, size, step, 0)

    return start, wait


def attend_kernel(
    heads, group, plan_ref, sq_ref, target_ref, page_ref, q_ref, pt_ref, len_ref, k_hbm, v_hbm,
    o_ref, ml_ref, lab_ref, sqsum_ref, vin_ref, sin_ref,
    keys, values, lim, limx, vt, s_buf, qx, stage, asked, queried, told, told_in,
    plans, sqs, table, tables, sems_kv, sems_plan, sems_sq, sems_q, sems_v, sems_s,
):
    ni = lax.axis_size("inst")
    me = lax.axis_index("inst")
    me_tp = lax.axis_index("tp")
    key_heads, pool, page, hd = keys.shape
    req = q_ref.shape[1]
    nx = qx.shape[1]
    scale = LOG2E / math.sqrt(hd)

    def fetch(g, which):
        source, target = ((k_hbm, keys), (v_hbm, values))[which]
        return pltpu.make_async_copy(source.at[:, g], target.at[g], sems_kv.at[which, g])

    for g in range(key_heads):
        fetch(g, 0).start()
        fetch(g, 1).start()
    greet(("inst", "tp"))
    start_plan, wait_plan = exchange("inst", lambda p: plan_ref, plans, sems_plan.at[0], sems_plan.at[1])
    start_sq, wait_sq = exchange("tp", lambda p: sq_ref, sqs, sems_sq.at[0], sems_sq.at[1])
    start_q, wait_q = exchange("inst", lambda p: asked.at[p], queried, sems_q.at[0], sems_q.at[1])
    start_v, wait_v = exchange("inst", lambda p: told.at[p], told_in, sems_v.at[0], sems_v.at[1])
    start_s, wait_s = exchange("inst", lambda p: table, tables, sems_s.at[0], sems_s.at[1])
    start_plan()
    start_sq()
    plans[me] = plan_ref[...]
    sqs[me_tp] = sq_ref[...]

    first = lax.broadcasted_iota(jnp.int32, pt_ref.shape, 0) * page
    room = jnp.clip(len_ref[...] - first, 0, page).astype(F32)
    column = lax.broadcasted_iota(jnp.int32, (1, nx), 1)
    owner = lax.rem(column, ni)
    wanted = jnp.full((1, nx), -1, jnp.int32)
    for m in range(target_ref.shape[0]):
        wanted = jnp.where(owner == target_ref[m], page_ref[m], wanted)
    wanted = jnp.where(column < group * ni, wanted, -1)
    for p in range(pool):
        lim[p : p + 1, :] = jnp.sum(jnp.where(pt_ref[...] == p, room, 0.0), axis=0, keepdims=True)
        limx[p : p + 1, :] = jnp.where(wanted == p, float(page), 0.0)
    vt[:, hd:, :] = jnp.ones((key_heads, vt.shape[1] - hd, vt.shape[2]), BF16)
    stage[...] = jnp.zeros_like(stage)
    table[...] = jnp.zeros_like(table)
    qx[...] = jnp.zeros_like(qx)

    pages = 4 if pool % 4 == 0 else 1
    span = pages * page
    chunks = pool // pages
    tokens = lax.broadcasted_iota(jnp.int32, (page, 128), 0).astype(F32)
    pair = 2 if group % 2 == 0 else 1

    def attend(g, blocks, limits, finish):
        state = {}

        def first_pass(i, ci):
            qs = blocks[i]()
            width = qs.shape[0]
            rows = keys[g, ci * pages : (ci + 1) * pages].reshape(span, hd)
            s = lax.dot_general(rows, qs, (((1,), (1,)), ((), ())), preferred_element_type=F32)
            highs = state.get(i)
            if highs is None:
                highs = [jnp.full((8, 128), LOWEST, F32) for _ in range(width // 128)]
            for pp in range(pages):
                p = ci * pages + pp
                usable = tokens < limits(i, p)
                for w in range(width // 128):
                    part = jnp.where(
                        usable, s[pp * page : (pp + 1) * page, w * 128 : (w + 1) * 128], MASKED
                    )
                    s_buf[i % 2, p * page : (p + 1) * page, w * 128 : (w + 1) * 128] = part
                    high = jnp.max(part.reshape(page // 8, 8, 128), axis=0)
                    highs[w] = jnp.maximum(highs[w], high)
            state[i] = highs

        for ci in range(chunks):
            first_pass(0, ci)
        for i in range(len(blocks)):
            tops = jnp.concatenate(
                [jnp.max(high, axis=0, keepdims=True) for high in state[i]], axis=1
            ) * scale
            total = None
            for ci in range(chunks):
                if i + 1 < len(blocks):
                    first_pass(i + 1, ci)
                rows = slice(ci * span, (ci + 1) * span)
                weights = jnp.exp2(s_buf[i % 2, rows, : tops.shape[1]] * scale - tops)
                part = jnp.dot(vt[g, :, rows], weights.astype(BF16), preferred_element_type=F32)
                total = part if total is None else total + part
            finish(i, total[:hd], total[hd : hd + 1, :], tops)

    def attend_own(g):
        def finish(i, total, sums, tops):
            columns = slice(i * pair * 128, (i + 1) * pair * 128)
            o_ref[g, :, columns] = total
            ml_ref[g, 0:1, columns] = tops
            ml_ref[g, 1:2, columns] = sums

        blocks = [
            lambda j=j: q_ref[pl.ds(g * group + j * pair, pair)].reshape(pair * req, hd)
            for j in range(group // pair)
        ]
        attend(g, blocks, lambda i, p: lim[p : p + 1, :], finish)

    def attend_asked(g):
        def finish(j, total, sums, tops):
            safe = jnp.maximum(sums, 1e-30)
            mean = (total / safe).T
            for q in range(group):
                lo = max(q * ni, j * 128)
                hi = min((q + 1) * ni, (j + 1) * 128)
                if lo < hi:
                    stage[lo - q * ni : hi - q * ni, g * group + q, :] = mean[lo - j * 128 : hi - j * 128]
            level = tops + jnp.log(safe) * LOG2E
            table[g : g + 1, j * 128 : (j + 1) * 128] = level

        blocks = [lambda j=j: qx[g, j * 128 : (j + 1) * 128, :] for j in range(nx // 128)]
        attend(g, blocks, lambda j, p: limx[p : p + 1, j * 128 : (j + 1) * 128], finish)

    def turn_values(g):
        for p in range(pool):
            vt[g, :hd, p * page : (p + 1) * page] = values[g, p].T

    def ask():
        wait_plan()
        mine = plans[:, 0, :] == me.astype(F32)
        label = jnp.sum(jnp.where(mine, plans[:, 1, :] + 1.0, 0.0), axis=1, keepdims=True) - 1.0
        lanes = lax.broadcasted_iota(jnp.int32, (ni, req), 1).astype(F32)
        lab_ref[...] = jnp.broadcast_to(label, lab_ref.shape)
        pick = jnp.where(label == lanes, 1.0, 0.0).astype(BF16)
        for h in range(heads):
            stage[:, h, :] = jnp.dot(pick, q_ref[h], preferred_element_type=F32)
        asked[...] = stage[...].astype(BF16)
        start_q()
        queried[me] = asked[me]

    def answer():
        wait_q()
        stage[...] = queried[...].astype(F32)
        for g in range(key_heads):
            for q in range(group):
                qx[g, q * ni : (q + 1) * ni, :] = stage[:, g * group + q, :].astype(BF16)
        for g in range(key_heads):
            attend_asked(g)
        told[...] = stage[...].astype(BF16)
        start_v()
        start_s()
        told_in[me] = told[me]
        tables[me] = table[...]

    def own(g, carry):
        for which in range(2):
            fetch(g, which).wait()
        turn_values(g)
        attend_own(g)

        @pl.when(g == 0)
        def _():
            ask()

        return carry

    early = min(2, key_heads)
    lax.fori_loop(0, early, own, 0)
    for g in range(early, key_heads):
        for which in range(2):
            fetch(g, which).wait()
        turn_values(g)
    answer()

    def rest(g, carry):
        attend_own(g)
        return carry

    lax.fori_loop(early, key_heads, rest, 0)
    wait_sq()
    sqsum_ref[...] = jnp.sum(sqs[...], axis=0)
    wait_v()
    wait_s()
    vin_ref[...] = told_in[...].astype(F32)
    sin_ref[...] = tables[...]


def join_kernel(
    features, group, heads, me_ref, vin_ref, sin_ref, lab_ref, o_ref, ml_ref, q_ref, proj_ref,
    sq_ref, len_ref, out_ref, kv_ref,
):
    ni, nx = sin_ref.shape[0], sin_ref.shape[2]
    hd = q_ref.shape[2]
    req = q_ref.shape[1]
    half = hd // 2
    scale = LOG2E / math.sqrt(hd)
    me = me_ref[0]
    inverse = jnp.broadcast_to(lax.rsqrt(sq_ref[0:1, :] / features + EPSILON), (hd, req)).T
    lane = lax.broadcasted_iota(jnp.int32, (1, hd), 1)
    step = lax.rem(lane, half).astype(F32)
    frequency = jnp.exp(step * (-2.0 / hd * math.log(ROPE_BASE)))
    angles = jnp.broadcast_to(len_ref[...].astype(F32), (hd, req)).T * frequency
    cosine = jnp.cos(angles)
    sine = jnp.sin(angles) * jnp.where(lane < half, -1.0, 1.0)
    lanes = lax.broadcasted_iota(jnp.int32, (ni, req), 1).astype(F32)
    owned = lab_ref[...] == lanes
    columns = lax.broadcasted_iota(jnp.int32, (ni, nx), 1)
    ones = jnp.ones((16, 3 * hd), BF16)
    for g in range(heads // group):
        x = proj_ref[g, :, :hd] * inverse
        rotated = (x * cosine + pltpu.roll(x, half, 1) * sine).astype(BF16)
        value = (proj_ref[g, :, hd:] * inverse).astype(BF16)
        kv_ref[:, 2 * g * hd : (2 * g + 1) * hd] = rotated
        kv_ref[:, (2 * g + 1) * hd : (2 * g + 2) * hd] = value
        key = rotated.astype(F32)
        value_t = value.astype(F32).T
        for q in range(group):
            h = g * group + q
            tile = slice(q * req, (q + 1) * req)
            product = q_ref[h].astype(F32) * key
            high = product.astype(BF16)
            rest = product - high.astype(F32)
            middle = rest.astype(BF16)
            low = (rest - middle.astype(F32)).astype(BF16)
            fresh = lax.dot_general(
                ones, jnp.concatenate([high, middle, low], axis=1), (((1,), (1,)), ((), ())),
                preferred_element_type=F32,
            )[0:1] * scale
            level = jnp.sum(
                jnp.where(columns == q * ni + me, sin_ref[:, g, :], 0.0), axis=1, keepdims=True
            )
            moved = jnp.where(owned, level, MASKED)
            top = ml_ref[g, 0:1, tile]
            best = jnp.maximum(jnp.maximum(top, fresh), jnp.max(moved, axis=0, keepdims=True))
            local_factor = jnp.exp2(top - best)
            fresh_factor = jnp.exp2(fresh - best)
            moved_factor = jnp.where(owned, jnp.exp2(moved - best), 0.0)
            bottom = (
                local_factor * ml_ref[g, 1:2, tile]
                + fresh_factor
                + jnp.sum(moved_factor, axis=0, keepdims=True)
            )
            top_sum = (
                o_ref[g, :, tile] * local_factor
                + value_t * fresh_factor
                + lax.dot_general(
                    vin_ref[:, h, :].astype(BF16), moved_factor.astype(BF16),
                    (((0,), (0,)), ((), ())), preferred_element_type=F32,
                )
            )
            out_ref[:, h * hd : (h + 1) * hd] = (top_sum / bottom).T.astype(BF16)


def body(
    hidden_state, norm_gain, kv_weight, queries, pool_keys, pool_values,
    page_table, lengths, move_target, move_page, move_request,
):
    ni, nt = lax.axis_size("inst"), lax.axis_size("tp")
    req, heads, hd = queries.shape
    pool, key_heads, page, _ = pool_keys.shape
    group = heads // key_heads
    moves = move_page.shape[0]
    features = hidden_state.shape[1] * nt
    padded = -(-heads // 16) * 16
    nx = -(-group * ni // 128) * 128
    params = functools.partial(pltpu.CompilerParams, vmem_limit_bytes=VMEM_BYTES)
    vmem = pl.BlockSpec(memory_space=pltpu.VMEM)
    smem = pl.BlockSpec(memory_space=pltpu.SMEM)

    widened = hidden_state.astype(F32)
    squares = jnp.sum(widened * widened, axis=1)
    scaled = (widened * norm_gain.astype(F32)[None, :]).astype(BF16)
    partial = jnp.einsum("rf,fgc->grc", scaled, kv_weight, preferred_element_type=F32)
    projected = lax.psum_scatter(partial, "tp", scatter_dimension=0, tiled=True)

    by_head = jnp.transpose(queries, (1, 0, 2))
    plan = jnp.pad(
        jnp.stack([move_target[:, 0], move_request]).astype(F32),
        ((0, 6), (0, 128 - moves)),
        constant_values=-1.0,
    )
    sq_tile = jnp.broadcast_to(squares[None, :], (8, req))
    tokens = pool * page
    slots = pltpu.VMEM((ni, padded, hd), BF16)
    hbm = pl.BlockSpec(memory_space=pl.ANY)
    local, levels, label, sq_total, moved_in, levels_in = pl.pallas_call(
        functools.partial(attend_kernel, heads, group),
        out_shape=(
            jax.ShapeDtypeStruct((key_heads, hd, group * req), F32),
            jax.ShapeDtypeStruct((key_heads, 8, group * req), F32),
            jax.ShapeDtypeStruct((ni, req), F32),
            jax.ShapeDtypeStruct((8, req), F32),
            jax.ShapeDtypeStruct((ni, padded, hd), F32),
            jax.ShapeDtypeStruct((ni, 8, nx), F32),
        ),
        in_specs=[vmem, vmem, smem, smem, vmem, vmem, vmem, hbm, hbm],
        out_specs=(vmem,) * 6,
        scratch_shapes=[
            pltpu.VMEM((key_heads, pool, page, hd), BF16),
            pltpu.VMEM((key_heads, pool, page, hd), BF16),
            pltpu.VMEM((pool, req), F32),
            pltpu.VMEM((pool, nx), F32),
            pltpu.VMEM((key_heads, hd + 16, tokens), BF16),
            pltpu.VMEM((2, tokens, 256), F32),
            pltpu.VMEM((key_heads, nx, hd), BF16),
            pltpu.VMEM((ni, padded, hd), F32),
            slots,
            slots,
            slots,
            slots,
            pltpu.VMEM((ni, 8, 128), F32),
            pltpu.VMEM((nt, 8, req), F32),
            pltpu.VMEM((8, nx), F32),
            pltpu.VMEM((ni, 8, nx), F32),
            pltpu.SemaphoreType.DMA((2, key_heads)),
            pltpu.SemaphoreType.DMA((2, ni)),
            pltpu.SemaphoreType.DMA((2, nt)),
            pltpu.SemaphoreType.DMA((2, ni)),
            pltpu.SemaphoreType.DMA((2, ni)),
            pltpu.SemaphoreType.DMA((2, ni)),
        ],
        compiler_params=params(collective_id=0, has_side_effects=True),
        cost_estimate=pl.CostEstimate(
            flops=4 * heads * (req + ni) * tokens * hd,
            bytes_accessed=4 * pool_keys.size,
            transcendentals=heads * req * tokens,
        ),
        name="attend",
    )(
        plan, sq_tile, move_target[:, 0], move_page, by_head, page_table.T, lengths[None, :],
        pool_keys, pool_values,
    )

    me = lax.axis_index("inst").astype(jnp.int32).reshape(1)
    attention_out, new_kv = pl.pallas_call(
        functools.partial(join_kernel, features, group, heads),
        out_shape=(
            jax.ShapeDtypeStruct((req, heads * hd), BF16),
            jax.ShapeDtypeStruct((req, key_heads * 2 * hd), BF16),
        ),
        in_specs=[smem] + [vmem] * 9,
        out_specs=(vmem,) * 2,
        compiler_params=params(),
        name="join",
    )(
        me, moved_in, levels_in, label, local, levels, by_head, projected, sq_total,
        lengths[None, :],
    )
    return (attention_out, new_kv.reshape(req, key_heads, 2 * hd))


def solution(mesh):
    return jax.shard_map(
        body,
        mesh=mesh,
        in_specs=(
            P("inst", "tp"),
            P("tp"),
            P("tp", None, None),
            P("inst", "tp", None),
            P("inst", "tp", None, None),
            P("inst", "tp", None, None),
            P("inst", None),
            P("inst"),
            P("inst", None),
            P("inst"),
            P("inst"),
        ),
        out_specs=(P("inst", "tp"), P("inst", "tp", None)),
        check_vma=False,
    )
```

time: 84.4 us -> 64.1 us (0.76)
  Pallas kernels: 57 us -> 36.7 us
    pallas_call x3 -> x1, Pallas kernels: 45.5 us -> 28.6 us  [body(): pl.pallas_call(functools.partial(attend_kernel, heads, group), out_shape=...]
    pallas_call x1, Pallas kernels: 11.4 us -> 8.08 us  [body(): pl.pallas_call(functools.partial(join_kernel, features, group, heads), ou...]
  transfers between devices with their start and end apart: 1 -> 1, of which waited for: 0 -> 0; matrix products, arithmetic and copies ran while one was open for 3% -> 4% of each run, Pallas kernels for 54% -> 45%
where the time goes in v2:
time: 64.1 us; the launch traced here: 63.8 us
  Pallas kernels  36.7 us (57%)
  between operations  14.1 us (22%)
  matrix products  7.95 us (12%)
  local copies, waits for them, and re-layouts  4.11 us (6%)
  other arithmetic  0.94 us (1%)
    pallas_call x1, Pallas kernels, body(): pl.pallas_call(functools.partial(attend_kernel, heads, group), out_shape=...  28.6 us
    pallas_call x1, Pallas kernels, body(): pl.pallas_call(functools.partial(join_kernel, features, group, heads), ou...  8.08 us
    dot_general x1, matrix products, body(): jnp.einsum('rf,fgc->grc', scaled, kv_weight, preferred_element_type=F32)  7.95 us
    reshape x1, local copies, waits for them, and re-layouts, body(): return (attention_out, new_kv.reshape(req, key_heads, 2 * hd))  1.84 us
  transfers between devices with their start and end apart: 1, of which 0 were waited for; matrix products, arithmetic and copies ran while one was open for 4% of the time, Pallas kernels for 45%

profile of v2, /device:TPU:0, one launch (start us, length us, event | category | flops | bytes accessed | tf_op | source)
XLA Modules:
  0.0 63.8 jit_solution(12048282345500044312)
XLA Ops:
  7.2 0.0 reduce-scatter.2.cloned.1.call-start
  7.2 0.7 %convert_element_type.14 = f32[3072]{0:T(1024)S(1)} convert(bf16[3072]{0:T(1024)(128)(2,1)} %param.12) | non-fusion elementwise | flops 3072 | bytes 18432 | tf_op jit(solution)/shard_map/convert_element_type | solution.py:353
  7.9 0.0 copy-start.1
  7.9 8.0 %fusion.4 = f32[8,128,256]{2,1,0:T(8,128)} fusion(bf16[3072,8,256]{2,1,0:T(8,128)(2,1)} %param.13, bf16[128,3072]{1,0:T(8,128)(2,1)} %param.11, f32[3072]{0:T(1024)S(1)} %convert_element_type.14), kind=kOutput, calls=%fused_computation.6 | convolution fusion | flops 1611792384 | bytes 14430208 | tf_op jit(solution)/shard_map/rf,fgc->grc/dot_general | solution.py:354
  15.9 0.0 copy-start.2
  15.9 0.0 copy-start.3
  15.9 0.0 copy-start
  15.9 0.0 reduce-scatter.2.cloned.1.call-update
  15.9 0.0 copy-done.1
  15.9 1.1 %copy.20 = bf16[128,24,128]{2,0,1:T(8,128)(2,1)} copy(bf16[128,24,128]{2,1,0:T(8,128)(2,1)S(1)} %copy-done.1) | data formatting | bytes 1572864 | tf_op args[3]
  17.0 0.0 copy-done.2
  17.0 0.0 copy-done.3
  17.0 0.6 pad.4.plan_ref
  17.6 0.0 copy-done
  17.6 0.2 fusion.2
  17.8 0.6 broadcast_in_dim.4.sq_ref
  18.4 28.6 %attend.1 = (f32[4,128,768]{2,1,0:T(8,128)}, f32[4,8,768]{2,1,0:T(8,128)}, f32[16,128]{1,0:T(8,128)}, f32[8,128]{1,0:T(8,128)}, f32[16,32,128]{2,1,0:T(8,128)}, /*index=5*/f32[16,8,128]{2,1,0:T(8,128)}) custom-call(f32[8,128]{1,0:T(8,128)} %pad.4.plan_ref, f32[8,128]{1,0:T(8,128)} %broadcast_in_dim.4.sq_ref, s32[8]{0:T(128)} %bitcast.19, s32[8]{0:T(128)} %page_ref.1, ...), custom_call_target="tpu_custom_call" | custom-call | flops 4529848320 | bytes 5242880 | tf_op jit(solution)/shard_map/attend/pallas_call | solution.py:367
  47.1 0.0 reduce-scatter.2.cloned.1.call-done.proj_ref
  47.1 8.1 %join.1 = (bf16[128,3072]{1,0:T(8,128)(2,1)}, bf16[128,1024]{1,0:T(8,128)(2,1)}) custom-call(s32[1]{0:T(128)} %bitcast.me_ref, f32[16,32,128]{2,1,0:T(8,128)} %get-tuple-element.10.vin_ref, f32[16,8,128]{2,1,0:T(8,128)} %get-tuple-element.11.sin_ref, f32[16,128]{1,0:T(8,128)} %get-tuple-element.12.lab_ref, f32[4,128,768]{2,1,0:T(8,128)} %get-tuple-element.13.o_ref, ...), custom_call_target="tpu_custom_call" | custom-call | tf_op jit(solution)/shard_map/join/pallas_call | solution.py:416
  55.2 1.8 %reshape.13 = bf16[128,4,256]{2,1,0:T(4,128)(2,1)} reshape(bf16[128,1024]{1,0:T(8,128)(2,1)} %get-tuple-element.17) | data formatting | bytes 524288 | tf_op jit(solution)/shard_map/reshape | solution.py:430
  (1 shorter events, 0.0 us)
Async XLA Ops:
  7.2 39.9 %reduce-scatter.2.cloned.1.call-start = ((), (), s32[]{:S(2)}) async-start(), calls=%async_computation.1 | async-start | bytes 1572864 | tf_op jit(solution)/shard_map/reduce_scatter | solution.py:355
  7.9 8.0 %copy-start.1 = (bf16[128,24,128]{2,1,0:T(8,128)(2,1)S(1)}, bf16[128,24,128]{2,1,0:T(8,128)(2,1)}, u32[]{:S(2)}) copy-start(bf16[128,24,128]{2,1,0:T(8,128)(2,1)} %param.14) | copy-start | bytes 2359300
  15.9 1.1 %copy-start.2 = (s32[8]{0:T(128)S(1)}, s32[8]{0:T(128)}, u32[]{:S(2)}) copy-start(s32[8]{0:T(128)} %param.21) | copy-start | bytes 100
  15.9 1.1 %copy-start.3 = (s32[8,1]{0,1:T(1,128)S(1)}, s32[8,1]{0,1:T(1,128)}, u32[]{:S(2)}) copy-start(s32[8,1]{0,1:T(1,128)} %param.19) | copy-start | bytes 100
  15.9 1.7 %copy-start = (bf16[128,3072]{1,0:T(8,128)(2,1)S(1)}, bf16[128,3072]{1,0:T(8,128)(2,1)}, u32[]{:S(2)}) copy-start(bf16[128,3072]{1,0:T(8,128)(2,1)} %param.11) | copy-start | bytes 2359300
Sparse Core Ops, SparseCore 0:
  16.0 23.0 reduce-scatter.1

commit v3 on v2

--- a/solution.py
+++ b/solution.py
@@ -82,10 +82,10 @@
 
 
 def attend_kernel(
-    heads, group, plan_ref, sq_ref, target_ref, page_ref, q_ref, pt_ref, len_ref, k_hbm, v_hbm,
+    heads, group, to_ref, asks_ref, squares_ref, target_ref, page_ref, q_ref, pt_ref, len_ref, k_hbm, v_hbm,
     o_ref, ml_ref, lab_ref, sqsum_ref, vin_ref, sin_ref,
     keys, values, lim, limx, vt, s_buf, qx, stage, asked, queried, told, told_in,
-    plans, sqs, table, tables, sems_kv, sems_plan, sems_sq, sems_q, sems_v, sems_s,
+    plan_ref, sq_ref, plans, sqs, table, tables, sems_kv, sems_plan, sems_sq, sems_q, sems_v, sems_s,
 ):
     ni = lax.axis_size("inst")
     me = lax.axis_index("inst")
@@ -102,6 +102,11 @@
     for g in range(key_heads):
         fetch(g, 0).start()
         fetch(g, 1).start()
+    moves = to_ref.shape[1]
+    plan_ref[...] = jnp.full(plan_ref.shape, -1.0, F32)
+    plan_ref[0:1, :moves] = to_ref[...].astype(F32)
+    plan_ref[1:2, :moves] = asks_ref[...].astype(F32)
+    sq_ref[...] = jnp.broadcast_to(squares_ref[...], sq_ref.shape)
     greet(("inst", "tp"))
     start_plan, wait_plan = exchange("inst", lambda p: plan_ref, plans, sems_plan.at[0], sems_plan.at[1])
     start_sq, wait_sq = exchange("tp", lambda p: sq_ref, sqs, sems_sq.at[0], sems_sq.at[1])
@@ -340,7 +345,6 @@
     req, heads, hd = queries.shape
     pool, key_heads, page, _ = pool_keys.shape
     group = heads // key_heads
-    moves = move_page.shape[0]
     features = hidden_state.shape[1] * nt
     padded = -(-heads // 16) * 16
     nx = -(-group * ni // 128) * 128
@@ -355,12 +359,6 @@
     projected = lax.psum_scatter(partial, "tp", scatter_dimension=0, tiled=True)
 
     by_head = jnp.transpose(queries, (1, 0, 2))
-    plan = jnp.pad(
-        jnp.stack([move_target[:, 0], move_request]).astype(F32),
-        ((0, 6), (0, 128 - moves)),
-        constant_values=-1.0,
-    )
-    sq_tile = jnp.broadcast_to(squares[None, :], (8, req))
     tokens = pool * page
     slots = pltpu.VMEM((ni, padded, hd), BF16)
     hbm = pl.BlockSpec(memory_space=pl.ANY)
@@ -374,7 +372,7 @@
             jax.ShapeDtypeStruct((ni, padded, hd), F32),
             jax.ShapeDtypeStruct((ni, 8, nx), F32),
         ),
-        in_specs=[vmem, vmem, smem, smem, vmem, vmem, vmem, hbm, hbm],
+        in_specs=[vmem, vmem, vmem, smem, smem, vmem, vmem, vmem, hbm, hbm],
         out_specs=(vmem,) * 6,
         scratch_shapes=[
             pltpu.VMEM((key_heads, pool, page, hd), BF16),
@@ -389,6 +387,8 @@
             slots,
             slots,
             slots,
+            pltpu.VMEM((8, 128), F32),
+            pltpu.VMEM((8, req), F32),
             pltpu.VMEM((ni, 8, 128), F32),
             pltpu.VMEM((nt, 8, req), F32),
             pltpu.VMEM((8, nx), F32),
@@ -408,7 +408,7 @@
         ),
         name="attend",
     )(
-        plan, sq_tile, move_target[:, 0], move_page, by_head, page_table.T, lengths[None, :],
+        move_target.T, move_request[None, :], squares[None, :], move_target[:, 0], move_page, by_head, page_table.T, lengths[None, :],
         pool_keys, pool_values,
     )
 

time: 64.1 us -> 63.4 us (0.989)
  local copies, waits for them, and re-layouts: 4.11 us -> 2.94 us
  transfers between devices with their start and end apart: 1 -> 1, of which waited for: 0 -> 0; matrix products, arithmetic and copies ran while one was open for 4% -> 3% of each run, Pallas kernels for 45% -> 45%
where the time goes in v3:
time: 63.4 us; the launch traced here: 63.2 us
  Pallas kernels  36.7 us (58%)
  between operations  14.1 us (22%)
  matrix products  7.96 us (13%)
  local copies, waits for them, and re-layouts  2.94 us (5%)
  other arithmetic  1.45 us (2%)
    pallas_call x1, Pallas kernels, body(): pl.pallas_call(functools.partial(attend_kernel, heads, group), out_shape=...  28.6 us
    pallas_call x1, Pallas kernels, body(): pl.pallas_call(functools.partial(join_kernel, features, group, heads), ou...  8.08 us
    dot_general x1, matrix products, body(): jnp.einsum('rf,fgc->grc', scaled, kv_weight, preferred_element_type=F32)  7.96 us
    reshape x1, local copies, waits for them, and re-layouts, body(): return (attention_out, new_kv.reshape(req, key_heads, 2 * hd))  1.84 us
  transfers between devices with their start and end apart: 1, of which 0 were waited for; matrix products, arithmetic and copies ran while one was open for 3% of the time, Pallas kernels for 45%

profile of v3, /device:TPU:0, one launch (start us, length us, event | category | flops | bytes accessed | tf_op | source)
XLA Modules:
  0.0 63.2 jit_solution(17567472376308898323)
XLA Ops:
  7.2 0.0 reduce-scatter.2.cloned.1.call-start
  7.2 0.7 %convert_element_type.10 = f32[3072]{0:T(1024)S(1)} convert(bf16[3072]{0:T(1024)(128)(2,1)} %param.12) | non-fusion elementwise | flops 3072 | bytes 18432 | tf_op jit(solution)/shard_map/convert_element_type | solution.py:357
  7.9 0.0 copy-start.1
  7.9 8.0 %fusion.4 = f32[8,128,256]{2,1,0:T(8,128)} fusion(bf16[3072,8,256]{2,1,0:T(8,128)(2,1)} %param.13, bf16[128,3072]{1,0:T(8,128)(2,1)} %param.11, f32[3072]{0:T(1024)S(1)} %convert_element_type.10), kind=kOutput, calls=%fused_computation.6 | convolution fusion | flops 1611792384 | bytes 14430208 | tf_op jit(solution)/shard_map/rf,fgc->grc/dot_general | solution.py:358
  15.9 0.0 copy-start
  15.9 0.0 reduce-scatter.2.cloned.1.call-update
  15.9 0.0 copy-done.1
  15.9 1.1 %copy.20 = bf16[128,24,128]{2,0,1:T(8,128)(2,1)} copy(bf16[128,24,128]{2,1,0:T(8,128)(2,1)S(1)} %copy-done.1) | data formatting | bytes 1572864 | tf_op args[3]
  17.0 0.0 copy-done
  17.0 0.8 %fusion.2 = f32[128]{0:T(128)} fusion(bf16[128,3072]{1,0:T(8,128)(2,1)S(1)} %copy-done), kind=kLoop, calls=%fused_computation.4 | loop fusion | flops 1179520 | bytes 786944 | tf_op jit(solution)/shard_map/reduce_sum | solution.py:356
  17.8 28.6 %attend.1 = (f32[4,128,768]{2,1,0:T(8,128)}, f32[4,8,768]{2,1,0:T(8,128)}, f32[16,128]{1,0:T(8,128)}, f32[8,128]{1,0:T(8,128)}, f32[16,32,128]{2,1,0:T(8,128)}, /*index=5*/f32[16,8,128]{2,1,0:T(8,128)}) custom-call(s32[1,8]{1,0:T(1,128)} %bitcast.21, s32[1,8]{1,0:T(1,128)} %bitcast.23, f32[1,128]{1,0:T(1,128)} %bitcast.19, s32[8]{0:T(128)} %bitcast.22, ...), custom_call_target="tpu_custom_call" | custom-call | flops 4529848320 | bytes 5242880 | tf_op jit(solution)/shard_map/attend/pallas_call | solution.py:365
  46.4 0.0 reduce-scatter.2.cloned.1.call-done.proj_ref
  46.4 8.1 %join.1 = (bf16[128,3072]{1,0:T(8,128)(2,1)}, bf16[128,1024]{1,0:T(8,128)(2,1)}) custom-call(s32[1]{0:T(128)} %bitcast.me_ref, f32[16,32,128]{2,1,0:T(8,128)} %get-tuple-element.10.vin_ref, f32[16,8,128]{2,1,0:T(8,128)} %get-tuple-element.11.sin_ref, f32[16,128]{1,0:T(8,128)} %get-tuple-element.12.lab_ref, f32[4,128,768]{2,1,0:T(8,128)} %get-tuple-element.13.o_ref, ...), custom_call_target="tpu_custom_call" | custom-call | tf_op jit(solution)/shard_map/join/pallas_call | solution.py:416
  54.5 1.8 %reshape.12 = bf16[128,4,256]{2,1,0:T(4,128)(2,1)} reshape(bf16[128,1024]{1,0:T(8,128)(2,1)} %get-tuple-element.17) | data formatting | bytes 524288 | tf_op jit(solution)/shard_map/reshape | solution.py:430
Async XLA Ops:
  7.2 39.2 %reduce-scatter.2.cloned.1.call-start = ((), (), s32[]{:S(2)}) async-start(), calls=%async_computation.1 | async-start | bytes 1572864 | tf_op jit(solution)/shard_map/reduce_scatter | solution.py:359
  7.9 8.0 %copy-start.1 = (bf16[128,24,128]{2,1,0:T(8,128)(2,1)S(1)}, bf16[128,24,128]{2,1,0:T(8,128)(2,1)}, u32[]{:S(2)}) copy-start(bf16[128,24,128]{2,1,0:T(8,128)(2,1)} %param.14) | copy-start | bytes 2359300
  15.9 1.1 %copy-start = (bf16[128,3072]{1,0:T(8,128)(2,1)S(1)}, bf16[128,3072]{1,0:T(8,128)(2,1)}, u32[]{:S(2)}) copy-start(bf16[128,3072]{1,0:T(8,128)(2,1)} %param.11) | copy-start | bytes 2359300
Sparse Core Ops, SparseCore 0:
  16.0 23.0 reduce-scatter.1
